TPU v7x, 256 devices: a whole 4x4x8 slice. The times are simulated.
256 devices in a mesh: tm: 64 (over x, z, core), chan: 4 (over y).
Axes of the slice: x: 4, y: 4, z: 8, core: 2. Of those that a mesh axis runs over, the one named last changes fastest.
Arguments:
- features: bfloat16 [393216, 512], P('tm', 'chan'), may hold values from -6 to 6
- snake_alpha: float32 [512], P('chan'), may hold values from 0.5 to 3
- down_weight: bfloat16 [512, 16, 1024], P(None, None, 'chan'), may hold values from -0.0625 to 0.0625
- grad_out: bfloat16 [49152, 1024], P('tm', 'chan'), may hold values from -6 to 6
Outputs:
- encoded: bfloat16 [49152, 1024], P('tm', 'chan')
- grad_features: bfloat16 [393216, 512], P('tm', 'chan')
- grad_down: bfloat16 [1024, 16, 512], P('tm', None, 'chan')
All inputs are finite; a program needn't handle non-finite values.
Results may differ from a plain program's by a relative error of at most 0.0049.
Values may be sent and summed in bfloat16 or wider, within the bound.
No kernel may reach another device: no remote copies, remote signals or barrier semaphores. Data moves between devices by JAX's collectives and lax.ppermute only.
A program may use at most 128 MiB of HBM per device.

v0:
```python
import math
import jax
import jax.numpy as jnp
from jax import lax
from jax.sharding import PartitionSpec as P

STRIDE = 8


def with_halo(block, sides, width):
    for axis, dim in sides:
        count = lax.axis_size(axis)
        forward = [(i, i + 1) for i in range(count - 1)]
        backward = [(target, source) for source, target in forward]
        low = lax.ppermute(
            lax.slice_in_dim(block, block.shape[dim] - width, None, axis=dim), axis, forward
        )
        high = lax.ppermute(lax.slice_in_dim(block, 0, width, axis=dim), axis, backward)
        block = jnp.concatenate([low, block, high], axis=dim)
    return block


def snake(values, alpha):
    return values + jnp.sin(alpha * values) ** 2 / alpha


def shards(features, snake_alpha, down_weight, grad_out):
    frames = features.shape[0]
    local_chans = features.shape[1]
    blocks_out = frames // STRIDE
    offset = STRIDE // 2
    wide = features.astype(jnp.float32)
    snaked = snake(wide, snake_alpha).astype(jnp.bfloat16)
    padded = with_halo(snaked, (("tm", 0),), offset)
    local_tiled = padded.reshape(blocks_out + 1, STRIDE, local_chans)
    full_cols = lax.all_gather(padded, "chan", axis=1, tiled=True)
    tiled = full_cols.reshape(blocks_out + 1, STRIDE, full_cols.shape[1])
    encoded = (
        jnp.einsum(
            "ujr,rjp->up", tiled[:-1], down_weight[:, :STRIDE], preferred_element_type=jnp.float32
        )
        + jnp.einsum(
            "ujr,rjp->up", tiled[1:], down_weight[:, STRIDE:], preferred_element_type=jnp.float32
        )
    ).astype(jnp.bfloat16)
    grad_pad = with_halo(grad_out, (("tm", 0),), 1)
    grad_full = lax.all_gather(grad_pad, "chan", axis=1, tiled=True)
    spread = jnp.einsum(
        "up,rjp->ujr", grad_pad[1:], down_weight[:, :STRIDE], preferred_element_type=jnp.float32
    ) + jnp.einsum(
        "up,rjp->ujr", grad_pad[:-1], down_weight[:, STRIDE:], preferred_element_type=jnp.float32
    )
    partial_terms = spread.reshape(frames + STRIDE, down_weight.shape[0])[offset : offset + frames]
    grad_snaked = lax.psum_scatter(partial_terms, "chan", scatter_dimension=1, tiled=True)
    grad_features = (grad_snaked * (1.0 + jnp.sin(2.0 * snake_alpha * wide))).astype(jnp.bfloat16)
    grad_inner = grad_full[1:-1]
    scale = 1.0 / math.sqrt(blocks_out * lax.axis_size("tm"))
    lower = jnp.einsum(
        "ujr,up->pjr", local_tiled[:-1], grad_inner, preferred_element_type=jnp.float32
    )
    upper = jnp.einsum(
        "ujr,up->pjr", local_tiled[1:], grad_inner, preferred_element_type=jnp.float32
    )
    summed = lax.psum_scatter(
        jnp.concatenate([lower, upper], axis=1), "tm", scatter_dimension=0, tiled=True
    )
    grad_down = (summed * scale).astype(jnp.bfloat16)
    return (encoded, grad_features, grad_down)


def solution(mesh):
    placed = (P("tm", "chan"), P("chan"), P(None, None, "chan"), P("tm", "chan"))
    return jax.shard_map(
        shards,
        mesh=mesh,
        in_specs=placed,
        out_specs=(P("tm", "chan"), P("tm", "chan"), P("tm", None, "chan")),
        check_vma=False,
    )
```

profile of v0, /device:TPU:8, one launch (start us, length us, event | category | flops | bytes accessed | tf_op | source)
XLA Modules:
  0.0 450.1 jit_solution(14186953188106699410)
XLA Ops:
  7.2 0.0 reduce-scatter.3.cloned.1.call-start
  7.2 0.7 fusion.51
  7.9 1.7 collective-permute-start.3
  9.7 0.0 copy-start.4
  9.7 1.4 collective-permute-start.2
  11.1 2.5 fusion.49
  13.6 0.0 copy-start
  13.6 0.0 copy-start.2
  13.6 0.0 collective-permute-done.3
  13.6 0.0 copy-done.4
  13.6 1.9 fusion.12
  15.5 0.0 copy-done
  15.5 0.0 collective-permute-done.2
  15.5 0.1 copy-done.2
  15.6 6.7 %add_bitcast_fusion = f32[769,8,512]{2,0,1:T(8,128)} fusion(f32[769,512,8]{1,0,2:T(8,128)S(1)} %fusion.12, bf16[512,8,256]{2,1,0:T(8,128)(2,1)S(1)} %get-tuple-element.11, bf16[1,256]{1,0:T(2,128)(2,1)S(1)} %collective-permute-done.2, bf16[768,256]{1,0:T(8,128)(2,1)S(1)} %copy-done.4), kind=kOutput, calls=%fused_computation | convolution fusion | flops 1616647168 | bytes 27689472 | tf_op jit(solution)/shard_map/up,rjp->ujr/dot_general | solution.py:48
  22.3 16.4 %copy.59 = f32[769,8,512]{2,1,0:T(8,128)} copy(f32[769,8,512]{2,0,1:T(8,128)} %add_bitcast_fusion) | data formatting | bytes 25198592 | tf_op jit(solution)/shard_map/add | solution.py:48
  38.8 10.9 %slice.76 = f32[6144,512]{1,0:T(8,128)} slice(f32[6152,512]{1,0:T(8,128)} %bitcast.31), slice={[4:6148], [0:512]} | slice | bytes 25165824 | tf_op jit(solution)/shard_map/slice | solution.py:53
  49.6 0.0 copy-start.6
  49.6 0.0 reduce-scatter.3.cloned.1.call-update
  49.7 0.0 copy-start.5
  49.7 0.0 all-gather.5.cloned.1.call-start
  49.7 0.2 copy.19
  49.9 0.1 copy.18
  50.0 0.1 copy.20
  50.2 1.0 pad_maximum_fusion.3
  51.2 0.0 all-gather.5.cloned.1.call-update
  51.2 0.0 all-gather.3.cloned.1.call-start
  51.3 0.0 copy-done.6
  51.3 121.0 %reduce-scatter.3.cloned.1.call-done = f32[6144,128]{1,0:T(8,128)} async-done(((f32[6144,512]{1,0:T(8,128)}), f32[6144,128]{1,0:T(8,128)}) %reduce-scatter.3.cloned.1.call-update) | async-done | bytes 3145744 | tf_op jit(solution)/shard_map/reduce_scatter | solution.py:54
  172.3 0.0 copy-done.5
  172.3 23.1 %fusion.11 = (bf16[6144,128]{1,0:T(8,128)(2,1)}, bf16[6144,128]{1,0:T(8,128)(2,1)S(1)}) fusion(f32[6144,128]{1,0:T(8,128)} %reduce-scatter.3.cloned.1.call-done, bf16[6144,128]{1,0:T(8,128)(2,1)S(1)} %copy-done.5, f32[128]{0:T(128)S(1)} %broadcast_multiply_fusion, f32[128]{0:T(128)S(1)} %copy-done.6), kind=kLoop, calls=%fused_computation.19 | loop fusion | flops 7864320 | bytes 7865344 | tf_op jit(solution)/shard_map/convert_element_type | solution.py:55
  195.3 1.8 collective-permute-start
  197.1 1.3 collective-permute-start.1
  198.4 0.0 collective-permute-done
  198.4 3.0 collective-permute-done.1
  201.4 8.7 %concatenate.21 = bf16[6152,128]{1,0:T(8,128)(2,1)} concatenate(bf16[4,128]{1,0:T(4,128)(2,1)S(1)} %collective-permute-done, bf16[6144,128]{1,0:T(8,128)(2,1)S(1)} %get-tuple-element.16, bf16[4,128]{1,0:T(4,128)(2,1)S(1)} %collective-permute-done.1), dimensions={0} | concatenate | bytes 3149824 | tf_op jit(solution)/shard_map/concatenate | solution.py:19
  210.1 0.0 all-gather.3.cloned.1.call-update
  210.1 0.0 reduce-scatter.5.cloned.1.call-start
  210.2 1.6 fusion.18
  211.8 0.0 all-gather.5.cloned.1.call-done
  211.8 0.0 copy-start.7
  211.8 3.9 fusion.21
  215.7 0.0 copy-done.7
  215.7 1.8 fusion.19
  217.6 3.8 pad_maximum_fusion
  221.4 0.0 reduce-scatter.5.cloned.1.call-update
  221.4 0.0 copy-start.1
  221.4 63.4 %all-gather.3.cloned.1.call-done = bf16[6152,512]{1,0:T(8,128)(2,1)} async-done(((bf16[6152,128]{1,0:T(8,128)(2,1)}), bf16[6152,512]{1,0:T(8,128)(2,1)}) %all-gather.3.cloned.1.call-update) | async-done | bytes 6299664 | tf_op jit(solution)/shard_map/all_gather | solution.py:36
  284.8 5.3 %slice_bitcast_fusion.1 = (bf16[768,8,512]{2,1,0:T(8,128)(2,1)S(1)}, bf16[768,8,512]{2,1,0:T(8,128)(2,1)S(1)}) fusion(bf16[6152,512]{1,0:T(8,128)(2,1)} %all-gather.3.cloned.1.call-done), kind=kLoop, calls=%fused_computation.4 | loop fusion | bytes 25165824 | tf_op jit(solution)/shard_map/slice | solution.py:40
  290.1 0.0 copy-done.1
  290.1 0.0 copy-start.3
  290.1 3.9 fusion.28
  294.1 0.0 copy-done.3
  294.1 4.7 %fusion.38 = bf16[768,256]{1,0:T(8,128)(2,1)} fusion(f32[768,256]{1,0:T(8,128)S(1)} %fusion.28, bf16[512,8,256]{2,1,0:T(8,128)(2,1)S(1)} %copy-done.3, bf16[768,8,512]{2,1,0:T(8,128)(2,1)S(1)} %get-tuple-element.9), kind=kOutput, calls=%fused_computation.37 | convolution fusion | flops 1611005952 | bytes 9568256 | tf_op jit(solution)/shard_map/ujr,rjp->up/dot_general | solution.py:39
  298.8 143.3 %reduce-scatter.5.cloned.1.call-done = f32[16,16,128]{2,0,1:T(8,128)} async-done(((f32[1024,16,128]{2,0,1:T(8,128)}), f32[16,16,128]{2,0,1:T(8,128)}) %reduce-scatter.5.cloned.1.call-update) | async-done | bytes 131088 | tf_op jit(solution)/shard_map/reduce_scatter | solution.py:64
  442.0 0.9 multiply_convert_fusion
  443.0 0.6 copy.23
  (2 shorter events, 0.0 us)
Async XLA Ops:
  7.2 165.1 %reduce-scatter.3.cloned.1.call-start = ((), (), s32[]{:S(2)}) async-start(), calls=%async_computation.3 | async-start | bytes 15728640 | tf_op jit(solution)/shard_map/reduce_scatter | solution.py:54
  7.9 5.7 %collective-permute-start.3 = (bf16[1,256]{1,0:T(2,128)(2,1)S(1)}, bf16[1,256]{1,0:T(2,128)(2,1)S(1)}, u32[]{:S(2)}, u32[]{:S(2)}) collective-permute-start(bf16[1,256]{1,0:T(2,128)(2,1)S(1)} %get-tuple-element.20), channel_id=1, source_target_pairs={{0,4},{4,8},{8,12},{12,16},{16,20},{20,24},{24,28},{28,32},{32,36}... | collective-permute-start | bytes 1544 | tf_op jit(solution)/shard_map/ppermute | solution.py:15
  9.7 4.0 copy-start.4
  9.7 5.9 %collective-permute-start.2 = (bf16[1,256]{1,0:T(2,128)(2,1)S(1)}, bf16[1,256]{1,0:T(2,128)(2,1)S(1)}, u32[]{:S(2)}, u32[]{:S(2)}) collective-permute-start(bf16[1,256]{1,0:T(2,128)(2,1)S(1)} %get-tuple-element.19), channel_id=1, source_target_pairs={{4,0},{8,4},{12,8},{16,12},{20,16},{24,20},{28,24},{32,28},{36,32}... | collective-permute-start | bytes 1544 | tf_op jit(solution)/shard_map/ppermute | solution.py:18
  13.6 1.9 copy-start
  13.6 2.0 copy-start.2
  49.6 1.6 copy-start.6
  49.7 122.6 %copy-start.5 = (bf16[6144,128]{1,0:T(8,128)(2,1)S(1)}, bf16[6144,128]{1,0:T(8,128)(2,1)}, u32[]{:S(2)}) copy-start(bf16[6144,128]{1,0:T(8,128)(2,1)} %param.4) | copy-start | bytes 4718596
  49.7 162.1 %all-gather.5.cloned.1.call-start = ((), (), s32[]{:S(2)}) async-start(), calls=%async_computation.4 | async-start | bytes 2293760 | tf_op jit(solution)/shard_map/all_gather | solution.py:47
  51.2 233.6 %all-gather.3.cloned.1.call-start = ((), (), s32[]{:S(2)}) async-start(), calls=%async_computation.2 | async-start | bytes 7874560 | tf_op jit(solution)/shard_map/all_gather | solution.py:36
  195.3 3.1 collective-permute-start
  197.1 4.3 collective-permute-start.1
  210.1 231.9 %reduce-scatter.5.cloned.1.call-start = ((), (), s32[]{:S(2)}) async-start(), calls=%async_computation.5 | async-start | bytes 8519680 | tf_op jit(solution)/shard_map/reduce_scatter | solution.py:64
  211.8 3.9 copy-start.7
  221.4 68.7 %copy-start.1 = (bf16[512,8,256]{2,1,0:T(8,128)(2,1)S(1)}, bf16[512,8,256]{2,1,0:T(8,128)(2,1)}, u32[]{:S(2)}) copy-start(bf16[512,8,256]{2,1,0:T(8,128)(2,1)} %copy-done) | copy-start | bytes 6291460
  290.1 3.9 copy-start.3
Sparse Core Ops, SparseCore 0:
  49.8 122.4 reduce-scatter.2
  174.1 31.2 all-gather.4
  210.3 74.5 all-gather.2
  288.9 153.1 reduce-scatter.4
where the time goes:
time: 451 us; the launch traced here: 450 us
  waiting for transfers between devices  331 us (73%)
  local copies, waits for them, and re-layouts  45.7 us (10%)
  other arithmetic  30.4 us (7%)
  matrix products  23 us (5%)
  between operations  14 us (3%)
  starting transfers between devices  6.38 us (1%)
    reduce_scatter x1, waiting for transfers between devices, shards(): lax.psum_scatter(jnp.concatenate([lower, upper], axis=1), 'tm', scatter_d...  143 us
    reduce_scatter x1, waiting for transfers between devices, shards(): lax.psum_scatter(partial_terms, 'chan', scatter_dimension=1, tiled=True)  121 us
    all_gather x1, waiting for transfers between devices, shards(): full_cols = lax.all_gather(padded, 'chan', axis=1, tiled=True)  63.4 us
    convert_element_type x1, other arithmetic, shards(): (grad_snaked * (1.0 + jnp.sin(2.0 * snake_alpha * wide))).astype(jnp.bflo...  23.1 us
    add x1, local copies, waits for them, and re-layouts, shards(): jnp.einsum('up,rjp->ujr', grad_pad[1:], down_weight[:, :STRIDE], preferre...  16.4 us
    slice x1, local copies, waits for them, and re-layouts, shards(): spread.reshape(frames + STRIDE, down_weight.shape[0])  10.9 us
  transfers between devices with their start and end apart: 8, of which 4 were waited for; matrix products, arithmetic and copies ran while one was open for 14% of the time, Pallas kernels for 0%

commit v1 on v0

--- a/solution.py
+++ b/solution.py
@@ -33,7 +33,12 @@
     snaked = snake(wide, snake_alpha).astype(jnp.bfloat16)
     padded = with_halo(snaked, (("tm", 0),), offset)
     local_tiled = padded.reshape(blocks_out + 1, STRIDE, local_chans)
-    full_cols = lax.all_gather(padded, "chan", axis=1, tiled=True)
+    ring = [padded]
+    for hop in range(3):
+        ring.append(lax.ppermute(ring[-1], "chan", [(dev, (dev + 1) % 4) for dev in range(4)]))
+    full_cols = jnp.roll(
+        jnp.concatenate(ring[::-1], axis=1), (lax.axis_index("chan") + 1) * ring[0].shape[1], axis=1
+    )
     tiled = full_cols.reshape(blocks_out + 1, STRIDE, full_cols.shape[1])
     encoded = (
         jnp.einsum(

time: 451 us -> 379 us (0.84)
  waiting for transfers between devices: 331 us -> 235 us
  local copies, waits for them, and re-layouts: 45.7 us -> 61.6 us
  starting transfers between devices: 6.38 us -> 11.4 us
    reduce_scatter x1, waiting for transfers between devices: 143 us -> 17.5 us  [shards(): lax.psum_scatter(jnp.concatenate([lower, upper], axis=1), 'tm', scatter_d...]
    ppermute x0 -> x3, waiting for transfers between devices: none -> 98.1 us  [shards(): lax.ppermute(ring[-1], 'chan', [(dev, (dev + 1) % 4) for dev in range(4)])]
    all_gather x1 -> x0, waiting for transfers between devices: 63.4 us -> none  [shards(): full_cols = lax.all_gather(padded, 'chan', axis=1, tiled=True)]
    unnamed x18 -> x27, local copies, waits for them, and re-layouts: 0.92 us -> 16.4 us
    concatenate x1, local copies, waits for them, and re-layouts: 8.69 us -> 2.58 us  [with_halo(): block = jnp.concatenate([low, block, high], axis=dim)]
    slice x1, local copies, waits for them, and re-layouts: 5.28 us -> 10.4 us  [shards(): tiled[:-1]]
  transfers between devices with their start and end apart: 8 -> 10, of which waited for: 4 -> 6; matrix products, arithmetic and copies ran while one was open for 14% -> 22% of each run, Pallas kernels for 0% -> 0%
where the time goes in v1:
time: 379 us
  waiting for transfers between devices  235 us (62%)
  local copies, waits for them, and re-layouts  61.6 us (16%)
  other arithmetic  30.9 us (8%)
  matrix products  26 us (7%)
  between operations  13.9 us (4%)
  starting transfers between devices  11.4 us (3%)
    reduce_scatter x1, waiting for transfers between devices, shards(): lax.psum_scatter(partial_terms, 'chan', scatter_dimension=1, tiled=True)  119 us
    ppermute x3, waiting for transfers between devices, shards(): lax.ppermute(ring[-1], 'chan', [(dev, (dev + 1) % 4) for dev in range(4)])  98.1 us
    convert_element_type x1, other arithmetic, shards(): (grad_snaked * (1.0 + jnp.sin(2.0 * snake_alpha * wide))).astype(jnp.bflo...  23.1 us
    reduce_scatter x1, waiting for transfers between devices, shards(): lax.psum_scatter(jnp.concatenate([lower, upper], axis=1), 'tm', scatter_d...  17.5 us
    unnamed x27, local copies, waits for them, and re-layouts  16.4 us
    add x1, local copies, waits for them, and re-layouts, shards(): jnp.einsum('up,rjp->ujr', grad_pad[1:], down_weight[:, :STRIDE], preferre...  16.4 us
    slice x1, local copies, waits for them, and re-layouts, shards(): spread.reshape(frames + STRIDE, down_weight.shape[0])  10.9 us
    slice x1, local copies, waits for them, and re-layouts, shards(): tiled[:-1]  10.4 us
  transfers between devices with their start and end apart: 10, of which 6 were waited for; matrix products, arithmetic and copies ran while one was open for 22% of the time, Pallas kernels for 0%

profile of v1, /device:TPU:8, one launch (start us, length us, event | category | flops | bytes accessed | tf_op | source)
XLA Modules:
  0.0 378.9 jit_solution(18252492216030596628)
XLA Ops:
  7.2 0.0 reduce-scatter.3.cloned.1.call-start
  7.2 0.7 fusion.51
  7.9 1.3 collective-permute-start.5
  9.2 0.0 copy-start.5
  9.2 3.2 collective-permute-start.6
  12.4 2.5 fusion.49
  14.9 0.0 copy-start
  14.9 0.0 copy-start.2
  14.9 0.0 collective-permute-done.6
  14.9 0.0 copy-done.5
  14.9 1.9 fusion.12
  16.8 0.0 copy-done
  16.8 0.0 collective-permute-done.5
  16.8 0.1 copy-done.2
  16.9 6.7 %add_bitcast_fusion = f32[769,8,512]{2,0,1:T(8,128)} fusion(f32[769,512,8]{1,0,2:T(8,128)S(1)} %fusion.12, bf16[512,8,256]{2,1,0:T(8,128)(2,1)S(1)} %get-tuple-element.11, bf16[1,256]{1,0:T(2,128)(2,1)S(1)} %collective-permute-done.5, bf16[768,256]{1,0:T(8,128)(2,1)S(1)} %copy-done.5), kind=kOutput, calls=%fused_computation | convolution fusion | flops 1616647168 | bytes 27689472 | tf_op jit(solution)/shard_map/up,rjp->ujr/dot_general | solution.py:53
  23.6 16.4 %copy.59 = f32[769,8,512]{2,1,0:T(8,128)} copy(f32[769,8,512]{2,0,1:T(8,128)} %add_bitcast_fusion) | data formatting | bytes 25198592 | tf_op jit(solution)/shard_map/add | solution.py:53
  40.1 10.9 %slice.74 = f32[6144,512]{1,0:T(8,128)} slice(f32[6152,512]{1,0:T(8,128)} %bitcast.31), slice={[4:6148], [0:512]} | slice | bytes 25165824 | tf_op jit(solution)/shard_map/slice | solution.py:58
  50.9 0.0 copy-start.7
  50.9 0.0 reduce-scatter.3.cloned.1.call-update
  51.0 0.0 all-gather.2.cloned.1.call-start
  51.0 0.2 copy.19
  51.2 0.1 copy.18
  51.3 0.1 copy.20
  51.5 1.0 pad_maximum_fusion.3
  52.5 0.0 all-gather.2.cloned.1.call-update
  52.5 0.0 reduce-scatter.5.cloned.1.call-start
  52.6 0.0 copy-done.7
  52.6 118.7 %reduce-scatter.3.cloned.1.call-done = f32[6144,128]{1,0:T(8,128)} async-done(((f32[6144,512]{1,0:T(8,128)}), f32[6144,128]{1,0:T(8,128)}) %reduce-scatter.3.cloned.1.call-update) | async-done | bytes 3145744 | tf_op jit(solution)/shard_map/reduce_scatter | solution.py:59
  171.3 23.1 %fusion.11 = (bf16[6144,128]{1,0:T(8,128)(2,1)}, bf16[6144,128]{1,0:T(8,128)(2,1)S(1)}) fusion(f32[6144,128]{1,0:T(8,128)} %reduce-scatter.3.cloned.1.call-done, bf16[6144,128]{1,0:T(8,128)(2,1)} %param.4, f32[128]{0:T(128)S(1)} %broadcast_multiply_fusion, f32[128]{0:T(128)S(1)} %copy-done.7), kind=kLoop, calls=%fused_computation.19 | loop fusion | flops 7864320 | bytes 7865344 | tf_op jit(solution)/shard_map/convert_element_type | solution.py:60
  194.4 1.3 collective-permute-start.1
  195.7 3.0 collective-permute-start
  198.8 0.0 collective-permute-done.1
  198.8 0.8 collective-permute-done
  199.6 2.6 concatenate.27
  202.2 1.2 collective-permute-start.2
  203.4 2.0 fusion.18
  205.5 4.0 %fusion.21 = f32[1024,8,128]{2,0,1:T(8,128)S(1)} fusion(bf16[768,8,128]{2,1,0:T(8,128)(2,1)} %get-tuple-element.13, bf16[770,1024]{0,1:T(8,128)(2,1)} %all-gather.2.cloned.1.call-done), kind=kOutput, calls=%fused_computation.32 | convolution fusion | flops 1610612736 | bytes 7340032 | tf_op jit(solution)/shard_map/ujr,up->pjr/dot_general | solution.py:63
  209.4 0.0 copy-done.6
  209.4 0.0 copy-done.8
  209.4 1.9 fusion.19
  211.3 3.8 pad_maximum_fusion
  215.1 0.0 reduce-scatter.5.cloned.1.call-update
  215.1 24.4 %collective-permute-done.2 = bf16[6152,128]{1,0:T(8,128)(2,1)} collective-permute-done((bf16[6152,128]{1,0:T(8,128)(2,1)S(1)}, bf16[6152,128]{1,0:T(8,128)(2,1)}, u32[]{:S(2)}, u32[]{:S(2)}) %collective-permute-start.2) | collective-permute-done | bytes 1574944 | tf_op jit(solution)/shard_map/ppermute | solution.py:38
  239.5 1.2 collective-permute-start.3
  240.7 36.8 %collective-permute-done.3 = bf16[6152,128]{1,0:T(8,128)(2,1)S(1)} collective-permute-done((bf16[6152,128]{1,0:T(8,128)(2,1)}, bf16[6152,128]{1,0:T(8,128)(2,1)S(1)}, u32[]{:S(2)}, u32[]{:S(2)}) %collective-permute-start.3) | collective-permute-done | bytes 1574944 | tf_op jit(solution)/shard_map/ppermute | solution.py:38
  277.5 0.0 collective-permute-start.4
  277.5 36.9 %collective-permute-done.4 = bf16[6152,128]{1,0:T(8,128)(2,1)} collective-permute-done((bf16[6152,128]{1,0:T(8,128)(2,1)S(1)}, bf16[6152,128]{1,0:T(8,128)(2,1)}, u32[]{:S(2)}, u32[]{:S(2)}) %collective-permute-start.4) | collective-permute-done | bytes 1574944 | tf_op jit(solution)/shard_map/ppermute | solution.py:38
  314.4 2.9 constant_dynamic-update-slice_fusion.7
  317.3 1.4 constant_dynamic-update-slice_fusion.6
  318.7 2.8 constant_dynamic-update-slice_fusion.5
  321.6 1.4 constant_dynamic-update-slice_fusion.4
  322.9 2.8 constant_dynamic-update-slice_fusion.3
  325.7 1.4 constant_dynamic-update-slice_fusion.2
  327.1 2.8 constant_dynamic-update-slice_fusion.1
  329.9 1.3 constant_dynamic-update-slice_fusion
  331.3 10.4 %dynamic-slice_bitcast_fusion.1 = (bf16[768,8,512]{2,1,0:T(8,128)(2,1)}, bf16[768,8,512]{2,1,0:T(8,128)(2,1)}) fusion(bf16[6152,1024]{1,0:T(8,128)(2,1)} %constant_dynamic-update-slice_fusion, s32[]{:T(128)S(6)} %select_n.14, s32[]{:T(128)S(6)} %add.44), kind=kLoop, calls=%fused_computation.4 | loop fusion | bytes 25165832 | tf_op jit(solution)/shard_map/slice | solution.py:45
  341.7 0.0 copy-done.1
  341.7 7.0 %fusion.28 = f32[768,256]{1,0:T(8,128)S(1)} fusion(bf16[512,8,256]{2,1,0:T(8,128)(2,1)S(1)} %copy-done.1, bf16[768,8,512]{2,1,0:T(8,128)(2,1)} %get-tuple-element.10), kind=kOutput, calls=%fused_computation.35 | convolution fusion | flops 1610612736 | bytes 9175040 | tf_op jit(solution)/shard_map/ujr,rjp->up/dot_general | solution.py:47
  348.7 0.0 copy-done.3
  348.7 0.0 copy-done.4
  348.7 4.7 %fusion.38 = bf16[768,256]{1,0:T(8,128)(2,1)} fusion(f32[768,256]{1,0:T(8,128)S(1)} %fusion.28, bf16[512,8,256]{2,1,0:T(8,128)(2,1)S(1)} %copy-done.3, bf16[768,8,512]{2,1,0:T(8,128)(2,1)S(1)} %copy-done.4), kind=kOutput, calls=%fused_computation.37 | convolution fusion | flops 1611005952 | bytes 9568256 | tf_op jit(solution)/shard_map/ujr,rjp->up/dot_general | solution.py:44
  353.4 17.5 %reduce-scatter.5.cloned.1.call-done = f32[16,16,128]{2,0,1:T(8,128)} async-done(((f32[1024,16,128]{2,0,1:T(8,128)}), f32[16,16,128]{2,0,1:T(8,128)}) %reduce-scatter.5.cloned.1.call-update) | async-done | bytes 131088 | tf_op jit(solution)/shard_map/reduce_scatter | solution.py:69
  370.8 0.9 multiply_convert_fusion
  371.8 0.6 copy.23
  (8 shorter events, 0.0 us)
Async XLA Ops:
  7.2 164.1 %reduce-scatter.3.cloned.1.call-start = ((), (), s32[]{:S(2)}) async-start(), calls=%async_computation.2 | async-start | bytes 15728640 | tf_op jit(solution)/shard_map/reduce_scatter | solution.py:59
  7.9 8.9 %collective-permute-start.5 = (bf16[1,256]{1,0:T(2,128)(2,1)S(1)}, bf16[1,256]{1,0:T(2,128)(2,1)S(1)}, u32[]{:S(2)}, u32[]{:S(2)}) collective-permute-start(bf16[1,256]{1,0:T(2,128)(2,1)S(1)} %get-tuple-element.19), channel_id=1, source_target_pairs={{4,0},{8,4},{12,8},{16,12},{20,16},{24,20},{28,24},{32,28},{36,32}... | collective-permute-start | bytes 1544 | tf_op jit(solution)/shard_map/ppermute | solution.py:18
  9.2 5.7 %copy-start.5 = (bf16[768,256]{1,0:T(8,128)(2,1)S(1)}, bf16[768,256]{1,0:T(8,128)(2,1)}, u32[]{:S(2)}) copy-start(bf16[768,256]{1,0:T(8,128)(2,1)} %param.7) | copy-start | bytes 1179652
  9.2 5.7 %collective-permute-start.6 = (bf16[1,256]{1,0:T(2,128)(2,1)S(1)}, bf16[1,256]{1,0:T(2,128)(2,1)S(1)}, u32[]{:S(2)}, u32[]{:S(2)}) collective-permute-start(bf16[1,256]{1,0:T(2,128)(2,1)S(1)} %get-tuple-element.20), channel_id=1, source_target_pairs={{0,4},{4,8},{8,12},{12,16},{16,20},{20,24},{24,28},{28,32},{32,36}... | collective-permute-start | bytes 1544 | tf_op jit(solution)/shard_map/ppermute | solution.py:15
  14.9 1.9 copy-start
  14.9 2.0 copy-start.2
  50.9 1.7 copy-start.7
  51.0 154.5 %all-gather.2.cloned.1.call-start = ((), (), s32[]{:S(2)}) async-start(), calls=%async_computation.3 | async-start | bytes 2293760 | tf_op jit(solution)/shard_map/all_gather | solution.py:52
  52.5 318.3 %reduce-scatter.5.cloned.1.call-start = ((), (), s32[]{:S(2)}) async-start(), calls=%async_computation.4 | async-start | bytes 8519680 | tf_op jit(solution)/shard_map/reduce_scatter | solution.py:69
  194.4 4.3 %collective-permute-start.1 = (bf16[4,128]{1,0:T(4,128)(2,1)S(1)}, bf16[4,128]{1,0:T(4,128)(2,1)S(1)}, u32[]{:S(2)}, u32[]{:S(2)}) collective-permute-start(bf16[4,128]{1,0:T(4,128)(2,1)S(1)} %get-tuple-element.17), channel_id=1, source_target_pairs={{4,0},{8,4},{12,8},{16,12},{20,16},{24,20},{28,24},{32,28},{36,32}... | collective-permute-start | bytes 3080 | tf_op jit(solution)/shard_map/ppermute | solution.py:18
  195.7 3.8 %collective-permute-start = (bf16[4,128]{1,0:T(4,128)(2,1)S(1)}, bf16[4,128]{1,0:T(4,128)(2,1)S(1)}, u32[]{:S(2)}, u32[]{:S(2)}) collective-permute-start(bf16[4,128]{1,0:T(4,128)(2,1)S(1)} %get-tuple-element.18), channel_id=1, source_target_pairs={{0,4},{4,8},{8,12},{12,16},{16,20},{20,24},{24,28},{28,32},{32,36}... | collective-permute-start | bytes 3080 | tf_op jit(solution)/shard_map/ppermute | solution.py:15
  202.2 37.3 %collective-permute-start.2 = (bf16[6152,128]{1,0:T(8,128)(2,1)S(1)}, bf16[6152,128]{1,0:T(8,128)(2,1)}, u32[]{:S(2)}, u32[]{:S(2)}) collective-permute-start(bf16[6152,128]{1,0:T(8,128)(2,1)S(1)} %concatenate.27), channel_id=1, source_target_pairs={{0,1},{1,2},{2,3},{3,0},{4,5},{5,6},{6,7},{7,4},{8,9},{9,10},{10,1... | collective-permute-start | bytes 4724744 | tf_op jit(solution)/shard_map/ppermute | solution.py:38
  205.5 4.0 %copy-start.6 = (bf16[768,8,128]{2,1,0:T(8,128)(2,1)S(1)}, bf16[768,8,128]{2,1,0:T(8,128)(2,1)}, u32[]{:S(2)}) copy-start(bf16[768,8,128]{2,1,0:T(8,128)(2,1)} %get-tuple-element.14) | copy-start | bytes 4718596
  205.5 4.0 %copy-start.8 = (bf16[770,1024]{0,1:T(8,128)(2,1)S(1)}, bf16[770,1024]{0,1:T(8,128)(2,1)}, u32[]{:S(2)}) copy-start(bf16[770,1024]{0,1:T(8,128)(2,1)} %all-gather.2.cloned.1.call-done) | copy-start | bytes 4730884
  239.5 38.0 %collective-permute-start.3 = (bf16[6152,128]{1,0:T(8,128)(2,1)}, bf16[6152,128]{1,0:T(8,128)(2,1)S(1)}, u32[]{:S(2)}, u32[]{:S(2)}) collective-permute-start(bf16[6152,128]{1,0:T(8,128)(2,1)} %collective-permute-done.2), channel_id=1, source_target_pairs={{0,1},{1,2},{2,3},{3,0},{4,5},{5,6},{6,7},{7,4},{8,9},{9,10},{10,1... | collective-permute-start | bytes 4724744 | tf_op jit(solution)/shard_map/ppermute | solution.py:38
  277.5 36.9 %collective-permute-start.4 = (bf16[6152,128]{1,0:T(8,128)(2,1)S(1)}, bf16[6152,128]{1,0:T(8,128)(2,1)}, u32[]{:S(2)}, u32[]{:S(2)}) collective-permute-start(bf16[6152,128]{1,0:T(8,128)(2,1)S(1)} %collective-permute-done.3), channel_id=1, source_target_pairs={{0,1},{1,2},{2,3},{3,0},{4,5},{5,6},{6,7},{7,4},{8,9},{9,10},{10,1... | collective-permute-start | bytes 4724744 | tf_op jit(solution)/shard_map/ppermute | solution.py:38
  331.3 10.4 %copy-start.1 = (bf16[512,8,256]{2,1,0:T(8,128)(2,1)S(1)}, bf16[512,8,256]{2,1,0:T(8,128)(2,1)}, u32[]{:S(2)}) copy-start(bf16[512,8,256]{2,1,0:T(8,128)(2,1)} %copy-done) | copy-start | bytes 6291460
  341.7 7.0 %copy-start.3 = (bf16[512,8,256]{2,1,0:T(8,128)(2,1)S(1)}, bf16[512,8,256]{2,1,0:T(8,128)(2,1)}, u32[]{:S(2)}) copy-start(bf16[512,8,256]{2,1,0:T(8,128)(2,1)} %copy-done.2) | copy-start | bytes 6291460
  341.7 7.0 %copy-start.4 = (bf16[768,8,512]{2,1,0:T(8,128)(2,1)S(1)}, bf16[768,8,512]{2,1,0:T(8,128)(2,1)}, u32[]{:S(2)}) copy-start(bf16[768,8,512]{2,1,0:T(8,128)(2,1)} %get-tuple-element.9) | copy-start | bytes 18874372
Sparse Core Ops, SparseCore 0:
  51.1 120.1 reduce-scatter.2
  173.1 31.2 all-gather.1
  215.2 155.5 reduce-scatter.4
